TPU v7x, 32 devices: a whole 2x2x4 slice. The times are simulated.
32 devices in a mesh: clips: 2 (over x), leaf: 16 (over z, y, core).
Axes of the slice: x: 2, y: 2, z: 4, core: 2. Of those that a mesh axis runs over, the one named last changes fastest.
Arguments:
- points: bfloat16 [131072, 64], P(('clips', 'leaf')), parts along dimension 0, may hold values from -6 to 6
- charges: bfloat16 [131072, 16], P(('clips', 'leaf')), parts along dimension 0, may hold values from -6 to 6
- near_list: int32 [256, 15], P(('clips', 'leaf')), parts along dimension 0, may hold values from 0 to 127, as said below
- near_count: int32 [256], P(('clips', 'leaf')), parts along dimension 0, may hold values from 1 to 15
- skel_index: int32 [32, 256], P(('clips', 'leaf')), parts along dimension 0, may hold values from 0 to 4095, as said below
- basis: bfloat16 [131072, 256], P(('clips', 'leaf')), parts along dimension 0, may hold values from -0.375 to 0.375
- upper_index: int32 [32, 2, 256], P(('clips', 'leaf')), parts along dimension 0, may hold values from 0 to 511, as said below
- upper_basis: bfloat16 [32, 2, 512, 256], P(('clips', 'leaf')), parts along dimension 0, as said below
- far_list: int32 [32, 2, 3], P(('clips', 'leaf')), parts along dimension 0, may hold values from -1 to 15, as said below
Outputs:
- product: float32 [131072, 16], P(('clips', 'leaf')), parts along dimension 0
There are 2 independent parts, one for each index of `clips`. A program takes and returns all parts, laid end to end along the dimension named above; each array names one. Nothing has to cross between parts.
Inputs may be any that keep to these rules, and one draw needn't show every extreme that they name: For s < near_count[a], near_list[a, s] are distinct leaves within 7 of a in increasing order, a among them; b is in a's list exactly when a is in b's; later slots hold a. `skel_index`: entry i lies in [i * 16, (i + 1) * 16). `upper_index`: entry i of a level is 2i or 2i + 1; rows of the devices of one node are equal. `upper_basis`: rows of the devices of one node are equal. `far_list`: entries of node j at level l are -1 or distinct nodes of that level among j - 3, j - 2, j + 2, j + 3 that are not children of the parent's non-neighbours (for even j: j - 2, j + 2, j + 3; for odd j: j - 3, j - 2, j + 2); rows of the devices of one node are equal.
All inputs are finite; a program needn't handle non-finite values.
Results may differ from a plain program's by a relative error of at most 0.0053.
Values may be sent and summed in bfloat16 or wider, within the bound.
No kernel may reach another device: no remote copies, remote signals or barrier semaphores. Data moves between devices by JAX's collectives and lax.ppermute only.
A program may use at most 64 MiB of HBM per device.

v0:
```python
import jax
import jax.numpy as jnp
from jax import lax
from jax.experimental import pallas as pl
from jax.experimental.pallas import tpu as pltpu
from jax.sharding import PartitionSpec as P

LEAF = 512
GROUP = 4
UNROLL = 4
CUTS = 4
CODE = 32
TOPS = 2
EXTRA = 16
VMEM = pl.BlockSpec(memory_space=pltpu.VMEM)
SMEM = pl.BlockSpec(memory_space=pltpu.SMEM)
LIMIT = 28 << 20
F32 = jnp.float32
BF16 = jnp.bfloat16


def dot(left, right):
    return jnp.dot(left, right, preferred_element_type=F32)


def dot_nt(left, right):
    return lax.dot_general(left, right, (((1,), (1,)), ((), ())), preferred_element_type=F32)


def dot_tn(left, right):
    return lax.dot_general(left, right, (((0,), (0,)), ((), ())), preferred_element_type=F32)


def norm_rows(feats, spread, ones_first):
    norm = jnp.sum(feats * feats, axis=0, keepdims=True) * (-1.0 / spread)
    high = norm.astype(BF16).astype(F32)
    mid = (norm - high).astype(BF16).astype(F32)
    low = norm - high - mid
    row = lax.broadcasted_iota(jnp.int32, (EXTRA, feats.shape[1]), 0)
    start = 3 if ones_first else 0
    rows = jnp.where((row >= 3 - start) & (row < 6 - start), 1.0, 0.0)
    for at, piece in enumerate((high, mid, low)):
        rows = jnp.where(row == start + at, piece, rows)
    return rows.astype(BF16)


def source_side(feats, spread):
    return jnp.concatenate([feats, norm_rows(feats.astype(F32), spread, False)], axis=0)


def target_side(feats, spread):
    feats_f = feats.astype(F32)
    scaled = (feats_f * (2.0 / spread)).astype(BF16)
    return jnp.concatenate([scaled, norm_rows(feats_f, spread, True)], axis=0)


def padded(rows, height):
    gap = height - rows.shape[0]
    return jnp.concatenate([rows, jnp.zeros((gap, rows.shape[1]), rows.dtype)], axis=0)


def one_hot(index, height, offset):
    rows = lax.broadcasted_iota(jnp.int32, (height, index.shape[1]), 0) + offset
    return jnp.where(rows == index, 1.0, 0.0).astype(BF16)


def chosen_first(upper, side, skeleton):
    half = skeleton // 2
    kept = upper[0, 0:1, pl.ds(pl.multiple_of(side * half, half), half)] - side * skeleton
    pair = lax.broadcasted_iota(jnp.int32, kept.shape, 1)
    order = jnp.concatenate([kept, 4 * pair + 1 - kept], axis=1)
    return one_hot(order, skeleton, 0)


def points_kernel(pts, skel, upper, out, own):
    me = lax.axis_index("leaf")
    side = lax.rem(me, 2)
    child = lax.rem(me // 2, 2)
    rows = pts.shape[1]
    skeleton = own.shape[1]
    half = rows // 2
    lanes = skeleton // 2
    picks = [
        dot(
            pts[:, at * half : (at + 1) * half],
            one_hot(skel[:, at * lanes : (at + 1) * lanes], half, at * half),
        )
        for at in range(2)
    ]
    pts0 = jnp.concatenate(picks, axis=1).astype(BF16)
    own[...] = pts0
    out[0] = dot(pts0, chosen_first(upper, side, skeleton)).astype(BF16)
    pts1 = dot(pts0, one_hot(upper[0, 0:1], skeleton, side * skeleton)).astype(BF16)
    out[1] = pts1
    out[2] = dot(pts1, one_hot(upper[0, 1:2], skeleton, child * skeleton)).astype(BF16)


def weights_kernel(w, basis, upper, ubasis, points, out, block):
    me = lax.axis_index("leaf")
    side = lax.rem(me, 2)
    child = lax.rem(me // 2, 2)
    rhs = w.shape[0]
    skeleton = basis.shape[1]
    w0 = dot(w[...], basis[...]).astype(BF16)
    low = pl.multiple_of(side * skeleton, skeleton)
    w1 = dot(w0, ubasis[0, 0, pl.ds(low, skeleton), :]).astype(BF16)
    up = pl.multiple_of(child * skeleton, skeleton)
    w2 = dot(w1, ubasis[0, 1, pl.ds(up, skeleton), :]).astype(BF16)
    block[0, 0:rhs] = dot(w0, chosen_first(upper, side, skeleton)).astype(BF16)
    block[1, 0:rhs] = w1
    block[2, 0:rhs] = w2
    block[:, rhs:] = points[...]

    def send(to, carry):
        near = jnp.abs(to // 2 - me // 2) == 1
        away = jnp.abs(to // GROUP - me // GROUP) >= 2
        out[to] = block[jnp.where(near, 0, jnp.where(away, 2, 1))]
        return carry

    lax.fori_loop(0, out.shape[0], send, 0)


def note_pairs(near, count, first, leaves, lists, starts):
    ends = tuple(jnp.int32(start) for start in starts)
    for leaf in range(leaves):

        def note(slot, ends, leaf=leaf):
            b = near[leaf, slot] - first
            after = []
            for end, (to, wanted) in zip(ends, lists):
                keep, place = wanted(leaf, b)
                to[end] = place + leaf * CODE
                after.append(end + keep.astype(jnp.int32))
            return tuple(after)

        ends = lax.fori_loop(0, count[leaf], note, ends)
    for end, (to, _) in zip(ends, lists):
        for at in range(UNROLL):
            to[end + at] = leaves * CODE
    return ends


def over_pairs(todo, length, unroll, work):
    def decoded(start, span):
        codes = [todo[start + at] for at in range(span)]
        return [(code // CODE, lax.rem(code, CODE)) for code in codes]

    def step(at, carry):
        work(decoded(at * unroll, unroll))
        return carry

    rounds = (length + 1) // unroll
    lax.fori_loop(0, rounds, step, 0)
    done = rounds * unroll
    span = unroll // 2
    while span >= 2:
        fits = length - done > span - 2

        @pl.when(fits)
        def _(done=done, span=span):
            work(decoded(done, span))

        done = done + jnp.where(fits, span, 0)
        span //= 2


def halo_place(b, leaves, held):
    return jnp.where(b < 0, b + held, jnp.maximum(b - leaves, 0))


def inside_kernel(
    near, count, held_in, mate_in, out, held, mate, target, source, weights, acc, pairs, singles, sems
):
    rhs = weights.shape[1]
    feats, rows = held.shape[0] - rhs, held.shape[1]
    leaves = rows // LEAF
    spread = 0.5 * feats
    moves = ((held_in, held), (mate_in, mate))
    loads = [pltpu.make_async_copy(a, b, sems.at[at]) for at, (a, b) in enumerate(moves)]
    for load in loads:
        load.start()
    me = lax.axis_index("leaf")
    even = lax.rem(me, 2) == 0
    for leaf in range(leaves):
        singles[leaf] = leaf * CODE + leaf
    lengths = note_pairs(
        near, count, me * leaves, leaves,
        (
            (pairs, lambda a, b: ((b > a) & (b < leaves), jnp.clip(b, 0, leaves - 1))),
            (
                singles,
                lambda a, b: (
                    ((b < 0) != even) & ((b < 0) | (b >= leaves)),
                    halo_place(b, leaves, leaves) + leaves,
                ),
            ),
        ),
        (0, leaves),
    )
    acc[...] = jnp.zeros_like(acc)
    target[leaves] = jnp.zeros_like(target[leaves])
    loads[0].wait()
    for leaf in range(leaves):
        at = slice(leaf * LEAF, (leaf + 1) * LEAF)
        source[leaf] = padded(source_side(held[:feats, at], spread), source.shape[2]).T
        target[leaf] = padded(target_side(held[:feats, at], spread), target.shape[1])
        weights[leaf] = held[feats:, at]

    def tile(a, b):
        return jnp.exp(dot(source[b], target[a])).astype(BF16)

    def single(these):
        tiles = [tile(a, b) for a, b in these]
        for (a, b), t in zip(these, tiles):
            acc[a] += dot(weights[b], t)

    def pair(these):
        tiles = [tile(a, b) for a, b in these]
        for (a, b), t in zip(these, tiles):
            acc[a] += dot(weights[b], t)
            acc[b] += dot_nt(weights[a], t)

    weights[leaves] = jnp.zeros_like(weights[0])
    over_pairs(pairs, lengths[0], 2 * UNROLL, pair)
    loads[1].wait()
    for leaf in range(leaves):
        at = slice(leaf * LEAF, (leaf + 1) * LEAF)
        source[leaves + leaf] = padded(source_side(mate[:feats, at], spread), source.shape[2]).T
        weights[leaves + leaf] = mate[feats:, at]
    over_pairs(singles, lengths[1], 2 * UNROLL, single)
    for leaf in range(leaves):
        out[:, leaf * LEAF : (leaf + 1) * LEAF] = acc[leaf]


def outside_kernel(
    near, count, held_in, other_in, inside_in, out,
    held, other, inside, target, source, weights, acc, singles, sems,
):
    rhs, rows = inside.shape
    feats = held.shape[0] - rhs
    leaves = rows // LEAF
    spread = 0.5 * feats
    moves = ((held_in, held), (other_in, other), (inside_in, inside))
    loads = [pltpu.make_async_copy(a, b, sems.at[at]) for at, (a, b) in enumerate(moves)]
    for load in loads:
        load.start()
    me = lax.axis_index("leaf")
    even = lax.rem(me, 2) == 0
    lengths = note_pairs(
        near, count, me * leaves, leaves,
        (
            (
                singles,
                lambda a, b: (
                    ((b < 0) == even) & ((b < 0) | (b >= leaves)),
                    halo_place(b, leaves, leaves),
                ),
            ),
        ),
        (0,),
    )
    acc[leaves] = jnp.zeros_like(acc[leaves])
    target[leaves] = jnp.zeros_like(target[leaves])
    for load in loads:
        load.wait()
    for leaf in range(leaves):
        at = slice(leaf * LEAF, (leaf + 1) * LEAF)
        target[leaf] = padded(target_side(held[:feats, at], spread), target.shape[1])
        acc[leaf] = inside[:, at]
    for leaf in range(leaves):
        at = slice(leaf * LEAF, (leaf + 1) * LEAF)
        source[leaf] = padded(source_side(other[:feats, at], spread), source.shape[2]).T
        weights[leaf] = other[feats:, at]

    def single(these):
        tiles = [jnp.exp(dot(source[b], target[a])).astype(BF16) for a, b in these]
        for (a, b), t in zip(these, tiles):
            acc[a] += dot(weights[b], t)

    over_pairs(singles, lengths[0], 2 * UNROLL, single)
    for leaf in range(leaves):
        out[:, leaf * LEAF : (leaf + 1) * LEAF] = acc[leaf]


def downward_kernel(
    far, got, own, upper, ubasis_in, basis_in, near_in, out,
    ubasis, basis, near, done, in_sems, out_sems,
):
    me = lax.axis_index("leaf")
    side = lax.rem(me, 2)
    child = lax.rem(me // 2, 2)
    feats, skeleton = own.shape
    rhs = near.shape[0]
    halves = [pl.ds(pl.multiple_of(at * skeleton, skeleton), skeleton) for at in (side, child)]
    moves = [
        (ubasis_in.at[0, 1, halves[1]], ubasis.at[1]),
        (ubasis_in.at[0, 0, halves[0]], ubasis.at[0]),
        (near_in, near),
        (basis_in, basis),
    ]
    loads = [pltpu.make_async_copy(a, b, in_sems.at[at]) for at, (a, b) in enumerate(moves)]
    for load in loads:
        load.start()
    spread = 0.5 * feats
    slots = far.shape[2]

    def node(start, span):
        parts = got[start].astype(F32)
        for at in range(1, span):
            parts = parts + got[start + at].astype(F32)
        return parts[0:rhs], parts[rhs : rhs + feats].astype(BF16)

    def potential(aim, nodes):
        weights = [jnp.where(counts, w, 0.0).astype(BF16) for counts, w, _ in nodes]
        points = jnp.concatenate([p for _, _, p in nodes], axis=1)
        tile = jnp.exp(dot_tn(aim, source_side(points, spread))).astype(BF16)
        return dot_nt(jnp.concatenate(weights, axis=1), tile)

    def listed(level, aim):
        nodes = []
        for slot in range(slots):
            k = far[0, level, slot]
            nodes.append((k >= 0, *node(jnp.maximum(k, 0) * 2**level, 2**level)))
        return potential(aim, nodes)

    v0 = listed(0, target_side(own[...], spread))
    mine = node(me // 2 * 2, 2)[1]
    beside = me // GROUP * GROUP + 2 * (1 - child)
    half = skeleton // 2
    theirs = jnp.concatenate([got[beside + at, rhs:, :half] for at in range(2)], axis=1)
    lower = jnp.where(child == 0, mine, theirs)
    higher = jnp.where(child == 0, theirs, mine)
    joined = jnp.concatenate([lower, higher], axis=1)
    v1 = listed(1, target_side(mine, spread))
    aim = target_side(
        dot(joined, one_hot(upper[0, 1:2], 2 * skeleton, 0)).astype(BF16), spread
    )
    tops = got.shape[0] // GROUP
    top = me // GROUP
    gap = jnp.maximum(top - 1, 0)
    width = top + 2 - gap
    batch = min(tops - 2, TOPS)

    def some_tops(step, total):
        nodes = []
        for at in range(batch):
            place = step * batch + at
            k = place + jnp.where(place < gap, 0, width)
            nodes.append((k < tops, *node(jnp.minimum(k, tops - 1) * GROUP, GROUP)))
        return total + potential(aim, nodes)

    v2 = jnp.zeros((rhs, skeleton), F32)
    if tops - 2 == batch:
        v2 = some_tops(0, v2)
    else:
        v2 = lax.fori_loop(0, (tops - 2 + batch - 1) // batch, some_tops, v2)
    for load in loads:
        load.wait()
    z1 = v1 + dot_nt(v2.astype(BF16), ubasis[1])
    z0 = v0 + dot_nt(z1.astype(BF16), ubasis[0])
    z0 = z0.astype(BF16)
    part = near.shape[1] // CUTS
    copies = []
    for at in range(CUTS):
        cut = slice(at * part, (at + 1) * part)
        done[:, cut] = near[:, cut] + dot_nt(z0, basis[cut])
        lane = pl.ds(at * part, part)
        copy = pltpu.make_async_copy(done.at[:, lane], out.at[:, lane], out_sems.at[at])
        copy.start()
        copies.append(copy)
    for copy in copies:
        copy.wait()


def call(kernel, name, out, specs, scratch, flops, alias={}, outs=None, moved=1 << 20):
    return pl.pallas_call(
        kernel,
        out_shape=out,
        in_specs=specs,
        out_specs=jax.tree.map(lambda _: VMEM, out) if outs is None else outs,
        scratch_shapes=scratch,
        compiler_params=pltpu.CompilerParams(vmem_limit_bytes=LIMIT),
        cost_estimate=pl.CostEstimate(flops=flops, bytes_accessed=moved, transcendentals=0),
        input_output_aliases=alias,
        name=name,
    )


def per_device(
    points, charges, near_list, near_count, skel_index, basis, upper_index, upper_basis, far_list
):
    devices = lax.axis_size("leaf")
    rows, feats = points.shape
    rhs = charges.shape[1]
    skeleton = skel_index.shape[1]
    leaves = rows // LEAF
    depth = 128
    pts = points.T
    w = charges.T
    mates = [(i, i ^ 1) for i in range(devices)]
    bridge = [(i, i + 1) for i in range(1, devices - 1, 2)]
    bridge = bridge + [(b, a) for a, b in bridge]
    packed = jnp.concatenate([pts, w], axis=0)
    mate = lax.ppermute(packed, "leaf", mates)
    other = lax.ppermute(packed, "leaf", bridge)
    height = rhs + feats
    levels, own = call(
        points_kernel,
        "points",
        (
            jax.ShapeDtypeStruct((3, feats, skeleton), BF16),
            jax.ShapeDtypeStruct((feats, skeleton), BF16),
        ),
        [VMEM] * 3,
        [],
        int(1e9),
        moved=16 << 20,
    )(pts, skel_index, upper_index)
    sent = call(
        weights_kernel,
        "weights",
        jax.ShapeDtypeStruct((devices, height, skeleton), BF16),
        [VMEM] * 5,
        [pltpu.VMEM((3, height, skeleton), BF16)],
        int(1e9),
    )(w, basis, upper_index, upper_basis, levels)
    got = lax.all_to_all(sent, "leaf", 0, 0)
    todo = pltpu.SMEM((leaves * (near_list.shape[1] + 1) + UNROLL + 1,), jnp.int32)
    whole = pl.BlockSpec(memory_space=pl.ANY)
    field = jax.ShapeDtypeStruct((rhs, rows), F32)
    near = call(
        inside_kernel,
        "near_inside",
        field,
        [SMEM, SMEM, whole, whole],
        [
            pltpu.VMEM(packed.shape, BF16),
            pltpu.VMEM(packed.shape, BF16),
            pltpu.VMEM((leaves + 1, depth, LEAF), BF16),
            pltpu.VMEM((2 * leaves, LEAF, depth), BF16),
            pltpu.VMEM((2 * leaves, rhs, LEAF), BF16),
            pltpu.VMEM((leaves + 1, rhs, LEAF), F32),
            todo,
            todo,
            pltpu.SemaphoreType.DMA((2,)),
        ],
        int(8e9),
    )(near_list, near_count, packed, mate)
    near = call(
        outside_kernel,
        "near_outside",
        field,
        [SMEM, SMEM, whole, whole, whole],
        [
            pltpu.VMEM(packed.shape, BF16),
            pltpu.VMEM(packed.shape, BF16),
            pltpu.VMEM((rhs, rows), F32),
            pltpu.VMEM((leaves + 1, depth, LEAF), BF16),
            pltpu.VMEM((leaves, LEAF, depth), BF16),
            pltpu.VMEM((leaves, rhs, LEAF), BF16),
            pltpu.VMEM((leaves + 1, rhs, LEAF), F32),
            todo,
            pltpu.SemaphoreType.DMA((3,)),
        ],
        int(8e9),
    )(near_list, near_count, packed, other, near)
    field = call(
        downward_kernel,
        "downward",
        field,
        [SMEM, VMEM, VMEM, VMEM, whole, whole, whole],
        [
            pltpu.VMEM((2, skeleton, skeleton), BF16),
            pltpu.VMEM(basis.shape, BF16),
            pltpu.VMEM((rhs, rows), F32),
            pltpu.VMEM((rhs, rows), F32),
            pltpu.SemaphoreType.DMA((4,)),
            pltpu.SemaphoreType.DMA((CUTS,)),
        ],
        int(1e11),
        {6: 0},
        outs=whole,
        moved=0,
    )(far_list, got, own, upper_index, upper_basis, basis, near)
    return field.T


def solution(mesh):
    both = ("clips", "leaf")
    in_specs = (
        P(both, None),
        P(both, None),
        P(both, None),
        P(both),
        P(both, None),
        P(both, None),
        P(both, None, None),
        P(both, None, None, None),
        P(both, None, None),
    )
    return jax.shard_map(
        per_device, mesh=mesh, in_specs=in_specs, out_specs=P(both, None), check_vma=False
    )
```

profile of v0, /device:TPU:18, one launch (start us, length us, event | category | flops | bytes accessed | tf_op | source)
XLA Modules:
  0.0 39.4 jit_solution(3085418247871816670)
XLA Ops:
  0.0 0.0 copy-start
  0.0 0.0 copy-start.7
  0.0 0.0 copy-start.6
  0.0 1.2 %pad_maximum_fusion.held_in = bf16[80,4096]{1,0:T(8,128)(2,1)S(1)} fusion(bf16[16,4096]{1,0:T(8,128)(2,1)} %bitcast.5, bf16[64,4096]{1,0:T(8,128)(2,1)} %bitcast.3), kind=kLoop, calls=%fused_computation | loop fusion | flops 1310720 | bytes 1310720 | tf_op jit(solution)/shard_map/concatenate | solution.py:403
  1.2 0.0 copy-start.1
  1.2 0.0 copy-start.2
  1.2 0.0 copy-start.3
  1.3 0.1 collective-permute-start.1
  1.3 3.5 %collective-permute-start = (bf16[80,4096]{1,0:T(8,128)(2,1)S(1)}, bf16[80,4096]{1,0:T(8,128)(2,1)}, u32[]{:S(2)}, u32[]{:S(2)}) collective-permute-start(bf16[80,4096]{1,0:T(8,128)(2,1)S(1)} %pad_maximum_fusion.held_in), channel_id=1, source_target_pairs={{1,2},{3,4},{5,6},{7,8},{9,10},{11,12},{13,14},{2,1},{4,3},{6,5},{... | collective-permute-start | bytes 1966088 | tf_op jit(solution)/shard_map/ppermute | solution.py:405
  4.9 0.0 copy-done
  4.9 0.0 copy-done.7
  4.9 0.0 copy-done.6
  4.9 0.6 %points.1 = (bf16[3,64,256]{2,1,0:T(8,128)(2,1)S(1)}, bf16[64,256]{1,0:T(8,128)(2,1)S(1)}) custom-call(bf16[64,4096]{1,0:T(8,128)(2,1)S(1)} %bitcast.4, s32[1,256]{1,0:T(1,128)S(1)} %copy-done.7, s32[1,2,256]{2,1,0:T(2,128)S(1)} %copy-done.6), custom_call_target="tpu_custom_call" | custom-call | flops 1000000000 | bytes 16777216 | tf_op jit(solution)/shard_map/points/pallas_call | solution.py:407
  5.5 0.0 copy-done.1
  5.5 0.0 copy-done.2
  5.5 0.0 copy-done.3
  5.5 1.9 %weights.1 = bf16[16,80,256]{2,1,0:T(8,128)(2,1)} custom-call(bf16[16,4096]{1,0:T(8,128)(2,1)S(1)} %bitcast.6, bf16[4096,256]{1,0:T(8,128)(2,1)S(1)} %copy-done.2, s32[1,2,256]{2,1,0:T(2,128)S(1)} %copy-done.6, bf16[1,2,512,256]{3,2,1,0:T(8,128)(2,1)S(1)} %copy-done.3, bf16[3,64,256]{2,1,0:T(8,128)(2,1)S(1)} %get-tuple-element.7.points), custom_call_target="tpu_custom_call" | custom-call | flops 1000000000 | bytes 1048576 | tf_op jit(solution)/shard_map/weights/pallas_call | solution.py:419
  7.4 0.0 copy-start.5
  7.4 0.0 copy-start.9
  7.4 5.4 %all-to-all-start = ((bf16[16,80,256]{2,1,0:T(8,128)(2,1)}), bf16[16,80,256]{2,1,0:T(8,128)(2,1)S(1)}, u32[]{:S(2)}, u32[]{:S(2)}) async-start(bf16[16,80,256]{2,1,0:T(8,128)(2,1)} %weights.1), calls=%async_computation | async-start | bytes 1310720 | tf_op jit(solution)/shard_map/all_to_all | solution.py:427
  12.8 0.0 collective-permute-done.1.mate_in
  12.8 0.0 copy-done.5
  12.8 0.0 copy-done.9
  12.8 14.7 %near_inside.1.inside_in = f32[16,4096]{1,0:T(8,128)S(1)} custom-call(s32[8,15]{1,0:T(8,128)S(1)} %copy-done.5, s32[8]{0:T(128)S(1)} %copy-done.9, bf16[80,4096]{1,0:T(8,128)(2,1)S(1)} %pad_maximum_fusion.held_in, bf16[80,4096]{1,0:T(8,128)(2,1)} %collective-permute-done.1.mate_in), custom_call_target="tpu_custom_call" | custom-call | flops 8000000000 | bytes 1048576 | tf_op jit(solution)/shard_map/near_inside/pallas_call | solution.py:431
  27.5 0.0 copy-start.8
  27.5 0.0 collective-permute-done.other_in
  27.5 6.6 %near_outside.1.near_in = f32[16,4096]{1,0:T(8,128)} custom-call(s32[8,15]{1,0:T(8,128)S(1)} %copy-done.5, s32[8]{0:T(128)S(1)} %copy-done.9, bf16[80,4096]{1,0:T(8,128)(2,1)S(1)} %pad_maximum_fusion.held_in, bf16[80,4096]{1,0:T(8,128)(2,1)} %collective-permute-done.other_in, f32[16,4096]{1,0:T(8,128)S(1)} %near_inside.1.inside_in), custom_call_target="tpu_custom_call" | custom-call | flops 8000000000 | bytes 1048576 | tf_op jit(solution)/shard_map/near_outside/pallas_call | solution.py:449
  34.1 0.0 all-to-all-done.got
  34.1 0.0 copy-done.8
  34.1 0.0 copy-start.4
  34.1 1.0 %copy-done.4 = bf16[1,2,512,256]{3,2,1,0:T(8,128)(2,1)S(1)} copy-done((bf16[1,2,512,256]{3,2,1,0:T(8,128)(2,1)S(1)}, bf16[1,2,512,256]{3,2,1,0:T(8,128)(2,1)}, u32[]{:S(2)}) %copy-start.4) | copy-done | bytes 524312
  35.1 4.1 %downward.1 = f32[16,4096]{1,0:T(8,128)} custom-call(s32[1,2,3]{2,1,0:T(2,128)S(1)} %copy-done.8, bf16[16,80,256]{2,1,0:T(8,128)(2,1)S(1)} %all-to-all-done.got, bf16[64,256]{1,0:T(8,128)(2,1)S(1)} %get-tuple-element.8.own, s32[1,2,256]{2,1,0:T(2,128)S(1)} %copy-done.6, bf16[1,2,512,256]{3,2,1,0:T(8,128)(2,1)S(1)} %copy-done.4, ...), custom_call_target="tpu_custom_call", output_to_operand_aliasing={{}: (6, {})} | custom-call | flops 99999997952 | tf_op jit(solution)/shard_map/downward/pallas_call | solution.py:467
Async XLA Ops:
  0.0 4.9 %copy-start = (bf16[4096,64]{0,1:T(8,128)(2,1)S(1)}, bf16[4096,64]{0,1:T(8,128)(2,1)}, u32[]{:S(2)}) copy-start(bf16[4096,64]{0,1:T(8,128)(2,1)} %param.9) | copy-start | bytes 1572868
  0.0 4.9 %copy-start.7 = (s32[1,256]{1,0:T(1,128)S(1)}, s32[1,256]{1,0:T(1,128)}, u32[]{:S(2)}) copy-start(s32[1,256]{1,0:T(1,128)} %skel.1) | copy-start | bytes 3076
  0.0 4.9 %copy-start.6 = (s32[1,2,256]{2,1,0:T(2,128)S(1)}, s32[1,2,256]{2,1,0:T(2,128)}, u32[]{:S(2)}) copy-start(s32[1,2,256]{2,1,0:T(2,128)} %upper.5) | copy-start | bytes 6148
  1.2 4.3 %copy-start.1 = (bf16[4096,16]{0,1:T(8,128)(2,1)S(1)}, bf16[4096,16]{0,1:T(8,128)(2,1)}, u32[]{:S(2)}) copy-start(bf16[4096,16]{0,1:T(8,128)(2,1)} %param.10) | copy-start | bytes 393220
  1.2 4.3 %copy-start.2 = (bf16[4096,256]{1,0:T(8,128)(2,1)S(1)}, bf16[4096,256]{1,0:T(8,128)(2,1)}, u32[]{:S(2)}) copy-start(bf16[4096,256]{1,0:T(8,128)(2,1)} %basis_in.1) | copy-start | bytes 6291460
  1.2 4.3 %copy-start.3 = (bf16[1,2,512,256]{3,2,1,0:T(8,128)(2,1)S(1)}, bf16[1,2,512,256]{3,2,1,0:T(8,128)(2,1)}, u32[]{:S(2)}) copy-start(bf16[1,2,512,256]{3,2,1,0:T(8,128)(2,1)} %ubasis_in.1) | copy-start | bytes 1572868
  1.3 11.5 %collective-permute-start.1 = (bf16[80,4096]{1,0:T(8,128)(2,1)S(1)}, bf16[80,4096]{1,0:T(8,128)(2,1)}, u32[]{:S(2)}, u32[]{:S(2)}) collective-permute-start(bf16[80,4096]{1,0:T(8,128)(2,1)S(1)} %pad_maximum_fusion.held_in), channel_id=1, source_target_pairs={{0,1},{1,0},{2,3},{3,2},{4,5},{5,4},{6,7},{7,6},{8,9},{9,8},{10,11... | collective-permute-start | bytes 1966088 | tf_op jit(solution)/shard_map/ppermute | solution.py:404
  1.3 26.2 %collective-permute-start = (bf16[80,4096]{1,0:T(8,128)(2,1)S(1)}, bf16[80,4096]{1,0:T(8,128)(2,1)}, u32[]{:S(2)}, u32[]{:S(2)}) collective-permute-start(bf16[80,4096]{1,0:T(8,128)(2,1)S(1)} %pad_maximum_fusion.held_in), channel_id=1, source_target_pairs={{1,2},{3,4},{5,6},{7,8},{9,10},{11,12},{13,14},{2,1},{4,3},{6,5},{... | collective-permute-start | bytes 1966088 | tf_op jit(solution)/shard_map/ppermute | solution.py:405
  7.4 5.4 %copy-start.5 = (s32[8,15]{1,0:T(8,128)S(1)}, s32[8,15]{1,0:T(8,128)}, u32[]{:S(2)}) copy-start(s32[8,15]{1,0:T(8,128)} %near.3) | copy-start | bytes 1444
  7.4 5.4 %copy-start.9 = (s32[8]{0:T(128)S(1)}, s32[8]{0:T(128)}, u32[]{:S(2)}) copy-start(s32[8]{0:T(128)} %count.3) | copy-start | bytes 100
  7.4 26.7 %all-to-all-start = ((bf16[16,80,256]{2,1,0:T(8,128)(2,1)}), bf16[16,80,256]{2,1,0:T(8,128)(2,1)S(1)}, u32[]{:S(2)}, u32[]{:S(2)}) async-start(bf16[16,80,256]{2,1,0:T(8,128)(2,1)} %weights.1), calls=%async_computation | async-start | bytes 1310720 | tf_op jit(solution)/shard_map/all_to_all | solution.py:427
  27.5 6.6 %copy-start.8 = (s32[1,2,3]{2,1,0:T(2,128)S(1)}, s32[1,2,3]{2,1,0:T(2,128)}, u32[]{:S(2)}) copy-start(s32[1,2,3]{2,1,0:T(2,128)} %far.1) | copy-start | bytes 76
  34.1 1.0 %copy-start.4 = (bf16[1,2,512,256]{3,2,1,0:T(8,128)(2,1)S(1)}, bf16[1,2,512,256]{3,2,1,0:T(8,128)(2,1)}, u32[]{:S(2)}) copy-start(bf16[1,2,512,256]{3,2,1,0:T(8,128)(2,1)} %ubasis_in.1) | copy-start | bytes 1572868
where the time goes:
time: 39.6 us; the launch traced here: 39.4 us
  Pallas kernels  27.7 us (70%)
  starting transfers between devices  9.02 us (23%)
  other arithmetic  1.21 us (3%)
  local copies, waits for them, and re-layouts  1.08 us (3%)
    pallas_call x1, Pallas kernels, per_device(): call(inside_kernel, 'near_inside', field, [SMEM, SMEM, whole, whole], [pl...  14.7 us
    pallas_call x1, Pallas kernels, per_device(): call(outside_kernel, 'near_outside', field, [SMEM, SMEM, whole, whole, wh...  6.56 us
    all_to_all x1, starting transfers between devices, per_device(): got = lax.all_to_all(sent, 'leaf', 0, 0)  5.42 us
    pallas_call x1, Pallas kernels, per_device(): call(downward_kernel, 'downward', field, [SMEM, VMEM, VMEM, VMEM, whole,...  4.06 us
    ppermute x1, starting transfers between devices, per_device(): other = lax.ppermute(packed, 'leaf', bridge)  3.53 us
    pallas_call x1, Pallas kernels, per_device(): call(weights_kernel, 'weights', jax.ShapeDtypeStruct((devices, height, sk...  1.85 us
    concatenate x1, other arithmetic, per_device(): packed = jnp.concatenate([pts, w], axis=0)  1.21 us
    unnamed x20, local copies, waits for them, and re-layouts  1.08 us
  transfers between devices with their start and end apart: 3, of which 0 were waited for; matrix products, arithmetic and copies ran while one was open for 0% of the time, Pallas kernels for 60%

commit v1 on v0

--- a/solution.py
+++ b/solution.py
@@ -233,14 +233,14 @@
 
 
 def outside_kernel(
-    near, count, held_in, other_in, inside_in, out,
-    held, other, inside, target, source, weights, acc, singles, sems,
+    near, count, held, other_in, inside_in, out,
+    other, inside, target, source, weights, acc, singles, sems,
 ):
     rhs, rows = inside.shape
     feats = held.shape[0] - rhs
     leaves = rows // LEAF
     spread = 0.5 * feats
-    moves = ((held_in, held), (other_in, other), (inside_in, inside))
+    moves = ((inside_in, inside), (other_in, other))
     loads = [pltpu.make_async_copy(a, b, sems.at[at]) for at, (a, b) in enumerate(moves)]
     for load in loads:
         load.start()
@@ -261,12 +261,12 @@
     )
     acc[leaves] = jnp.zeros_like(acc[leaves])
     target[leaves] = jnp.zeros_like(target[leaves])
-    for load in loads:
-        load.wait()
+    loads[0].wait()
     for leaf in range(leaves):
         at = slice(leaf * LEAF, (leaf + 1) * LEAF)
         target[leaf] = padded(target_side(held[:feats, at], spread), target.shape[1])
         acc[leaf] = inside[:, at]
+    loads[1].wait()
     for leaf in range(leaves):
         at = slice(leaf * LEAF, (leaf + 1) * LEAF)
         source[leaf] = padded(source_side(other[:feats, at], spread), source.shape[2]).T
@@ -450,9 +450,8 @@
         outside_kernel,
         "near_outside",
         field,
-        [SMEM, SMEM, whole, whole, whole],
+        [SMEM, SMEM, VMEM, whole, whole],
         [
-            pltpu.VMEM(packed.shape, BF16),
             pltpu.VMEM(packed.shape, BF16),
             pltpu.VMEM((rhs, rows), F32),
             pltpu.VMEM((leaves + 1, depth, LEAF), BF16),
@@ -460,7 +459,7 @@
             pltpu.VMEM((leaves, rhs, LEAF), BF16),
             pltpu.VMEM((leaves + 1, rhs, LEAF), F32),
             todo,
-            pltpu.SemaphoreType.DMA((3,)),
+            pltpu.SemaphoreType.DMA((2,)),
         ],
         int(8e9),
     )(near_list, near_count, packed, other, near)

time: 39.6 us -> 38.9 us (0.982)
  the two profiles are of different devices: /device:TPU:18 before, /device:TPU:25 now
where the time goes in v1:
time: 38.9 us; the launch traced here: 39 us
  Pallas kernels  25.3 us (65%)
  starting transfers between devices  9.24 us (24%)
  waiting for transfers between devices  1.85 us (5%)
  other arithmetic  1.21 us (3%)
  local copies, waits for them, and re-layouts  1.08 us (3%)
    pallas_call x1, Pallas kernels, per_device(): call(inside_kernel, 'near_inside', field, [SMEM, SMEM, whole, whole], [pl...  11.8 us
    pallas_call x1, Pallas kernels, per_device(): call(outside_kernel, 'near_outside', field, [SMEM, SMEM, VMEM, whole, who...  7.05 us
    all_to_all x1, starting transfers between devices, per_device(): got = lax.all_to_all(sent, 'leaf', 0, 0)  5.31 us
    pallas_call x1, Pallas kernels, per_device(): call(downward_kernel, 'downward', field, [SMEM, VMEM, VMEM, VMEM, whole,...  4.06 us
    ppermute x1, starting transfers between devices, per_device(): other = lax.ppermute(packed, 'leaf', bridge)  3.18 us
    pallas_call x1, Pallas kernels, per_device(): call(weights_kernel, 'weights', jax.ShapeDtypeStruct((devices, height, sk...  1.85 us
    ppermute x1, waiting for transfers between devices, per_device(): other = lax.ppermute(packed, 'leaf', bridge)  1.85 us
    concatenate x1, other arithmetic, per_device(): packed = jnp.concatenate([pts, w], axis=0)  1.21 us
  transfers between devices with their start and end apart: 3, of which 1 were waited for; matrix products, arithmetic and copies ran while one was open for 0% of the time, Pallas kernels for 54%

profile of v1, /device:TPU:25, one launch (start us, length us, event | category | flops | bytes accessed | tf_op | source)
XLA Modules:
  0.0 39.0 jit_solution(17730788867257219980)
XLA Ops:
  0.0 0.0 copy-start
  0.0 0.0 copy-start.7
  0.0 0.0 copy-start.6
  0.0 1.2 %pad_maximum_fusion.held_in.held = bf16[80,4096]{1,0:T(8,128)(2,1)S(1)} fusion(bf16[16,4096]{1,0:T(8,128)(2,1)} %bitcast.5, bf16[64,4096]{1,0:T(8,128)(2,1)} %bitcast.3), kind=kLoop, calls=%fused_computation | loop fusion | flops 1310720 | bytes 1310720 | tf_op jit(solution)/shard_map/concatenate | solution.py:403
  1.2 0.0 copy-start.1
  1.2 0.0 copy-start.2
  1.2 0.0 copy-start.3
  1.3 0.7 %collective-permute-start.1 = (bf16[80,4096]{1,0:T(8,128)(2,1)S(1)}, bf16[80,4096]{1,0:T(8,128)(2,1)}, u32[]{:S(2)}, u32[]{:S(2)}) collective-permute-start(bf16[80,4096]{1,0:T(8,128)(2,1)S(1)} %pad_maximum_fusion.held_in.held), channel_id=1, source_target_pairs={{0,1},{1,0},{2,3},{3,2},{4,5},{5,4},{6,7},{7,6},{8,9},{9,8},{10,11... | collective-permute-start | bytes 1966088 | tf_op jit(solution)/shard_map/ppermute | solution.py:404
  2.0 3.2 %collective-permute-start = (bf16[80,4096]{1,0:T(8,128)(2,1)S(1)}, bf16[80,4096]{1,0:T(8,128)(2,1)}, u32[]{:S(2)}, u32[]{:S(2)}) collective-permute-start(bf16[80,4096]{1,0:T(8,128)(2,1)S(1)} %pad_maximum_fusion.held_in.held), channel_id=1, source_target_pairs={{1,2},{3,4},{5,6},{7,8},{9,10},{11,12},{13,14},{2,1},{4,3},{6,5},{... | collective-permute-start | bytes 1966088 | tf_op jit(solution)/shard_map/ppermute | solution.py:405
  5.2 0.0 copy-done
  5.2 0.0 copy-done.7
  5.2 0.0 copy-done.6
  5.2 0.6 %points.1 = (bf16[3,64,256]{2,1,0:T(8,128)(2,1)S(1)}, bf16[64,256]{1,0:T(8,128)(2,1)S(1)}) custom-call(bf16[64,4096]{1,0:T(8,128)(2,1)S(1)} %bitcast.4, s32[1,256]{1,0:T(1,128)S(1)} %copy-done.7, s32[1,2,256]{2,1,0:T(2,128)S(1)} %copy-done.6), custom_call_target="tpu_custom_call" | custom-call | flops 1000000000 | bytes 16777216 | tf_op jit(solution)/shard_map/points/pallas_call | solution.py:407
  5.8 0.0 copy-done.1
  5.8 0.0 copy-done.2
  5.8 0.0 copy-done.3
  5.8 1.9 %weights.1 = bf16[16,80,256]{2,1,0:T(8,128)(2,1)} custom-call(bf16[16,4096]{1,0:T(8,128)(2,1)S(1)} %bitcast.6, bf16[4096,256]{1,0:T(8,128)(2,1)S(1)} %copy-done.2, s32[1,2,256]{2,1,0:T(2,128)S(1)} %copy-done.6, bf16[1,2,512,256]{3,2,1,0:T(8,128)(2,1)S(1)} %copy-done.3, bf16[3,64,256]{2,1,0:T(8,128)(2,1)S(1)} %get-tuple-element.7.points), custom_call_target="tpu_custom_call" | custom-call | flops 1000000000 | bytes 1048576 | tf_op jit(solution)/shard_map/weights/pallas_call | solution.py:419
  7.7 0.0 copy-start.5
  7.7 0.0 copy-start.9
  7.7 5.3 %all-to-all-start = ((bf16[16,80,256]{2,1,0:T(8,128)(2,1)}), bf16[16,80,256]{2,1,0:T(8,128)(2,1)S(1)}, u32[]{:S(2)}, u32[]{:S(2)}) async-start(bf16[16,80,256]{2,1,0:T(8,128)(2,1)} %weights.1), calls=%async_computation | async-start | bytes 1310720 | tf_op jit(solution)/shard_map/all_to_all | solution.py:427
  13.0 0.0 collective-permute-done.1.mate_in
  13.0 0.0 copy-done.5
  13.0 0.0 copy-done.9
  13.0 11.8 %near_inside.1.inside_in = f32[16,4096]{1,0:T(8,128)S(1)} custom-call(s32[8,15]{1,0:T(8,128)S(1)} %copy-done.5, s32[8]{0:T(128)S(1)} %copy-done.9, bf16[80,4096]{1,0:T(8,128)(2,1)S(1)} %pad_maximum_fusion.held_in.held, bf16[80,4096]{1,0:T(8,128)(2,1)} %collective-permute-done.1.mate_in), custom_call_target="tpu_custom_call" | custom-call | flops 8000000000 | bytes 1048576 | tf_op jit(solution)/shard_map/near_inside/pallas_call | solution.py:431
  24.8 0.0 copy-start.8
  24.8 1.8 %collective-permute-done.other_in = bf16[80,4096]{1,0:T(8,128)(2,1)} collective-permute-done((bf16[80,4096]{1,0:T(8,128)(2,1)S(1)}, bf16[80,4096]{1,0:T(8,128)(2,1)}, u32[]{:S(2)}, u32[]{:S(2)}) %collective-permute-start) | collective-permute-done | bytes 655392 | tf_op jit(solution)/shard_map/ppermute | solution.py:405
  26.6 7.1 %near_outside.1.near_in = f32[16,4096]{1,0:T(8,128)} custom-call(s32[8,15]{1,0:T(8,128)S(1)} %copy-done.5, s32[8]{0:T(128)S(1)} %copy-done.9, bf16[80,4096]{1,0:T(8,128)(2,1)S(1)} %pad_maximum_fusion.held_in.held, bf16[80,4096]{1,0:T(8,128)(2,1)} %collective-permute-done.other_in, f32[16,4096]{1,0:T(8,128)S(1)} %near_inside.1.inside_in), custom_call_target="tpu_custom_call" | custom-call | flops 8000000000 | bytes 1048576 | tf_op jit(solution)/shard_map/near_outside/pallas_call | solution.py:449
  33.7 0.0 all-to-all-done.got
  33.7 0.0 copy-done.8
  33.7 0.0 copy-start.4
  33.7 1.0 %copy-done.4 = bf16[1,2,512,256]{3,2,1,0:T(8,128)(2,1)S(1)} copy-done((bf16[1,2,512,256]{3,2,1,0:T(8,128)(2,1)S(1)}, bf16[1,2,512,256]{3,2,1,0:T(8,128)(2,1)}, u32[]{:S(2)}) %copy-start.4) | copy-done | bytes 524312
  34.8 4.1 %downward.1 = f32[16,4096]{1,0:T(8,128)} custom-call(s32[1,2,3]{2,1,0:T(2,128)S(1)} %copy-done.8, bf16[16,80,256]{2,1,0:T(8,128)(2,1)S(1)} %all-to-all-done.got, bf16[64,256]{1,0:T(8,128)(2,1)S(1)} %get-tuple-element.8.own, s32[1,2,256]{2,1,0:T(2,128)S(1)} %copy-done.6, bf16[1,2,512,256]{3,2,1,0:T(8,128)(2,1)S(1)} %copy-done.4, ...), custom_call_target="tpu_custom_call", output_to_operand_aliasing={{}: (6, {})} | custom-call | flops 99999997952 | tf_op jit(solution)/shard_map/downward/pallas_call | solution.py:466
Async XLA Ops:
  0.0 5.2 %copy-start = (bf16[4096,64]{0,1:T(8,128)(2,1)S(1)}, bf16[4096,64]{0,1:T(8,128)(2,1)}, u32[]{:S(2)}) copy-start(bf16[4096,64]{0,1:T(8,128)(2,1)} %param.9) | copy-start | bytes 1572868
  0.0 5.2 %copy-start.7 = (s32[1,256]{1,0:T(1,128)S(1)}, s32[1,256]{1,0:T(1,128)}, u32[]{:S(2)}) copy-start(s32[1,256]{1,0:T(1,128)} %skel.1) | copy-start | bytes 3076
  0.0 5.2 %copy-start.6 = (s32[1,2,256]{2,1,0:T(2,128)S(1)}, s32[1,2,256]{2,1,0:T(2,128)}, u32[]{:S(2)}) copy-start(s32[1,2,256]{2,1,0:T(2,128)} %upper.5) | copy-start | bytes 6148
  1.2 4.6 %copy-start.1 = (bf16[4096,16]{0,1:T(8,128)(2,1)S(1)}, bf16[4096,16]{0,1:T(8,128)(2,1)}, u32[]{:S(2)}) copy-start(bf16[4096,16]{0,1:T(8,128)(2,1)} %param.10) | copy-start | bytes 393220
  1.2 4.6 %copy-start.2 = (bf16[4096,256]{1,0:T(8,128)(2,1)S(1)}, bf16[4096,256]{1,0:T(8,128)(2,1)}, u32[]{:S(2)}) copy-start(bf16[4096,256]{1,0:T(8,128)(2,1)} %basis_in.1) | copy-start | bytes 6291460
  1.2 4.6 %copy-start.3 = (bf16[1,2,512,256]{3,2,1,0:T(8,128)(2,1)S(1)}, bf16[1,2,512,256]{3,2,1,0:T(8,128)(2,1)}, u32[]{:S(2)}) copy-start(bf16[1,2,512,256]{3,2,1,0:T(8,128)(2,1)} %ubasis_in.1) | copy-start | bytes 1572868
  1.3 11.7 %collective-permute-start.1 = (bf16[80,4096]{1,0:T(8,128)(2,1)S(1)}, bf16[80,4096]{1,0:T(8,128)(2,1)}, u32[]{:S(2)}, u32[]{:S(2)}) collective-permute-start(bf16[80,4096]{1,0:T(8,128)(2,1)S(1)} %pad_maximum_fusion.held_in.held), channel_id=1, source_target_pairs={{0,1},{1,0},{2,3},{3,2},{4,5},{5,4},{6,7},{7,6},{8,9},{9,8},{10,11... | collective-permute-start | bytes 1966088 | tf_op jit(solution)/shard_map/ppermute | solution.py:404
  2.0 24.7 %collective-permute-start = (bf16[80,4096]{1,0:T(8,128)(2,1)S(1)}, bf16[80,4096]{1,0:T(8,128)(2,1)}, u32[]{:S(2)}, u32[]{:S(2)}) collective-permute-start(bf16[80,4096]{1,0:T(8,128)(2,1)S(1)} %pad_maximum_fusion.held_in.held), channel_id=1, source_target_pairs={{1,2},{3,4},{5,6},{7,8},{9,10},{11,12},{13,14},{2,1},{4,3},{6,5},{... | collective-permute-start | bytes 1966088 | tf_op jit(solution)/shard_map/ppermute | solution.py:405
  7.7 5.3 %copy-start.5 = (s32[8,15]{1,0:T(8,128)S(1)}, s32[8,15]{1,0:T(8,128)}, u32[]{:S(2)}) copy-start(s32[8,15]{1,0:T(8,128)} %near.3) | copy-start | bytes 1444
  7.7 5.3 %copy-start.9 = (s32[8]{0:T(128)S(1)}, s32[8]{0:T(128)}, u32[]{:S(2)}) copy-start(s32[8]{0:T(128)} %count.3) | copy-start | bytes 100
  7.7 26.0 %all-to-all-start = ((bf16[16,80,256]{2,1,0:T(8,128)(2,1)}), bf16[16,80,256]{2,1,0:T(8,128)(2,1)S(1)}, u32[]{:S(2)}, u32[]{:S(2)}) async-start(bf16[16,80,256]{2,1,0:T(8,128)(2,1)} %weights.1), calls=%async_computation | async-start | bytes 1310720 | tf_op jit(solution)/shard_map/all_to_all | solution.py:427
  24.8 8.9 %copy-start.8 = (s32[1,2,3]{2,1,0:T(2,128)S(1)}, s32[1,2,3]{2,1,0:T(2,128)}, u32[]{:S(2)}) copy-start(s32[1,2,3]{2,1,0:T(2,128)} %far.1) | copy-start | bytes 76
  33.7 1.0 %copy-start.4 = (bf16[1,2,512,256]{3,2,1,0:T(8,128)(2,1)S(1)}, bf16[1,2,512,256]{3,2,1,0:T(8,128)(2,1)}, u32[]{:S(2)}) copy-start(bf16[1,2,512,256]{3,2,1,0:T(8,128)(2,1)} %ubasis_in.1) | copy-start | bytes 1572868
